TPU v7x, 256 devices: a whole 4x4x8 slice. The times are simulated.
256 devices in a mesh: tm: 8 (over z_lo, core), height: 32 (over x, y, z_hi).
Axes of the slice: x: 4, y: 4, z: 8 (z_hi: 2, z_lo: 4; z = z_hi * 4 + z_lo), core: 2. Of those that a mesh axis runs over, the one named last changes fastest.
Arguments:
- clean_latents: bfloat16 [32, 128, 16, 3072], P('tm', 'height'), may hold values from -6 to 6
- gaussian_noise: bfloat16 [32, 128, 16, 3072], P('tm', 'height'), may hold values from -6 to 6
- text_states: bfloat16 [256, 3072], replicated, may hold values from -6 to 6
- queries: bfloat16 [32, 128, 16, 1536], P('tm', 'height'), may hold values from -40 to 40
- key_states: bfloat16 [32, 128, 16, 1536], P('tm', 'height'), may hold values from -8 to 8
- cotangent: bfloat16 [32, 128, 16, 1536], P('tm', 'height'), may hold values from -240 to 240
- text_keys: bfloat16 [256, 1536], replicated, may hold values from -6 to 6
- window_radii: int32 [12, 3], replicated, may hold values from 0 to 1
- timestep: int32 [1], replicated, may hold values from 200 to 799
- sketch_seed: int32 [1], replicated, may hold values from 0 to 65535
- down_image: bfloat16 [3072, 16], replicated, may hold values from -0.109375 to 0.109375
- up_image: bfloat16 [16, 1536], replicated, may hold values from -1.5 to 1.5
- down_text: bfloat16 [3072, 16], replicated, may hold values from -0.109375 to 0.109375
- up_text: bfloat16 [16, 1536], replicated, may hold values from -1.5 to 1.5
Outputs:
- value_grad: bfloat16 [32, 128, 16, 1536], P('tm', 'height')
- grad_sketch: float32 [16384], replicated
All inputs are finite; a program needn't handle non-finite values.
Results may differ from a plain program's by a relative error of at most 0.0075.
Values may be sent and summed in bfloat16 or wider, within the bound.
A program may use at most 128 MiB of HBM per device.

v0:
```python
import jax
import jax.numpy as jnp
from jax import lax
from jax.sharding import PartitionSpec as P

SKETCH = 16384
TW = 8


def padded_2(block, sides, width):
    for axis, dim in sides:
        count = lax.axis_size(axis)
        forward = [(i, i + 1) for i in range(count - 1)]
        backward = [(target, source) for source, target in forward]
        low = lax.ppermute(
            lax.slice_in_dim(block, block.shape[dim] - width, None, axis=dim), axis, forward
        )
        high = lax.ppermute(lax.slice_in_dim(block, 0, width, axis=dim), axis, backward)
        block = jnp.concatenate([low, block, high], axis=dim)
    return block


def shifted(array, axis, by):
    size = lax.axis_size(axis)
    pairs = [(i, i + by) for i in range(size) if 0 <= i + by < size]
    return lax.ppermute(array, axis, pairs)


def tile_rows(block, width):
    frame_count, row_count, col_count = (block.shape[0], block.shape[1], block.shape[2])
    rest = block.shape[3:]
    col_tiles = col_count // width
    shaped = block.reshape((frame_count, row_count, col_tiles, width) + rest)
    order = (2, 0, 1, 3) + tuple(range(4, 4 + len(rest)))
    return jnp.transpose(shaped, order).reshape((col_tiles, frame_count * row_count * width) + rest)


def region_rows(padded, width):
    col_count = padded.shape[2] - 2 * width
    views = [
        tile_rows(padded[:, :, shift_col * width : shift_col * width + col_count], width)
        for shift_col in range(3)
    ]
    return jnp.concatenate(views, axis=1)


def window_mask(
    radius, frame_tile, row_tile, frame_tiles, row_tiles, col_tiles, frame_count, row_count, width
):
    region = 27 * frame_count * row_count * width
    position = jnp.arange(region, dtype=jnp.int32)
    col_step = position // (9 * frame_count * row_count * width) - 1
    frame_step = position // (3 * row_count * width) % (3 * frame_count) // frame_count - 1
    row_step = position // width % (3 * row_count) // row_count - 1
    inside = (
        (jnp.abs(frame_step) <= radius[0])
        & (jnp.abs(row_step) <= radius[1])
        & (jnp.abs(col_step) <= radius[2])
    )
    inside = inside & (frame_tile + frame_step >= 0) & (frame_tile + frame_step < frame_tiles)
    inside = inside & (row_tile + row_step >= 0) & (row_tile + row_step < row_tiles)
    col_index = jnp.arange(col_tiles, dtype=jnp.int32)[:, None]
    return (
        inside[None, :]
        & (col_index + col_step[None, :] >= 0)
        & (col_index + col_step[None, :] < col_tiles)
    )


def forward_head(query_head, key_region, text_head, cot_head, allowed, score_scale):
    image_scores = (
        jnp.einsum("cqd,cld->cql", query_head, key_region, preferred_element_type=jnp.float32)
        * score_scale
    )
    image_scores = jnp.where(allowed[:, None, :], image_scores, -jnp.inf)
    text_scores = (
        jnp.einsum("cqd,td->cqt", query_head, text_head, preferred_element_type=jnp.float32)
        * score_scale
    )
    row_max = jnp.maximum(jnp.max(image_scores, axis=-1), jnp.max(text_scores, axis=-1))
    total = jnp.sum(jnp.exp(image_scores - row_max[..., None]), axis=-1) + jnp.sum(
        jnp.exp(text_scores - row_max[..., None]), axis=-1
    )
    log_total = row_max + jnp.log(total)
    text_probs = jnp.exp(text_scores - log_total[..., None]).astype(jnp.bfloat16)
    text_part = jnp.einsum("cqt,cqd->td", text_probs, cot_head, preferred_element_type=jnp.float32)
    return (image_scores, log_total, text_part)


def place_back(spread, frame_count, row_count, width):
    col_tiles, head_width = (spread.shape[0], spread.shape[2])
    shaped = spread.reshape(col_tiles, 3, 3 * frame_count, 3 * row_count, width, head_width)
    placed = jnp.zeros((3 * frame_count, 3 * row_count, col_tiles, width, head_width), jnp.float32)
    for shift_col in range(3):
        moved = jnp.transpose(shaped[:, shift_col], (1, 2, 0, 3, 4))
        moved = jnp.pad(moved, ((0, 0), (0, 0), (1, 1), (0, 0), (0, 0)))
        placed = placed + moved[:, :, 2 - shift_col : 2 - shift_col + col_tiles]
    return placed.reshape(3 * frame_count, 3 * row_count, col_tiles * width, head_width)


def sketch_signs(seed_value, rows, width):
    row_part = jnp.arange(rows, dtype=jnp.int32)[:, None] * width
    position = row_part + jnp.arange(width, dtype=jnp.int32)[None, :]
    mixed_bits = position * 1103515245 + seed_value * 12345 + 1013904223
    mixed_bits = mixed_bits ^ mixed_bits >> 16
    mixed_bits = mixed_bits * 73244475
    mixed_bits = mixed_bits ^ mixed_bits >> 16
    return (1 - 2 * (mixed_bits >> 7 & 1)).astype(jnp.float32)


def count_sketch(pieces, seed_value, width, sketch_scale):
    flat = jnp.concatenate([piece.reshape(-1) for piece in pieces]).reshape(-1, width)
    signed = flat * sketch_signs(seed_value, flat.shape[0], width)
    return jnp.sum(signed, axis=0) * sketch_scale


def text_grads(text_hidden, text_value, text_states, up_text):
    highest = lax.Precision.HIGHEST
    text_up_grad = jnp.dot(text_hidden.T, text_value, precision=highest)
    text_back = jnp.dot(text_value, up_text.astype(jnp.float32).T, precision=highest)
    text_down_grad = jnp.dot(text_states.astype(jnp.float32).T, text_back, precision=highest)
    return (text_down_grad, text_up_grad)


def per_device(
    clean_latents,
    gaussian_noise,
    text_states,
    queries,
    key_states,
    cotangent,
    text_keys,
    window_radii,
    timestep,
    sketch_seed,
    down_image,
    up_image,
    down_text,
    up_text,
):
    frame_count, row_count, col_count, value_width = queries.shape
    head_count = window_radii.shape[0]
    head_width = value_width // head_count
    col_tiles = col_count // TW
    score_scale = head_width ** (-0.5)
    frame_tile = lax.axis_index("tm")
    row_tile = lax.axis_index("height")
    frame_tiles = lax.axis_size("tm")
    row_tiles = lax.axis_size("height")
    pad_spec = ((0, 0), (0, 0), (TW, TW), (0, 0))
    key_pad = jnp.pad(padded_2(key_states, (("tm", 0), ("height", 1)), frame_count), pad_spec)
    own_q = tile_rows(queries, TW)
    own_c = tile_rows(cotangent, TW)
    head_ids = jnp.arange(head_count, dtype=jnp.int32)

    def head_mask(head_index):
        return window_mask(
            window_radii[head_index],
            frame_tile,
            row_tile,
            frame_tiles,
            row_tiles,
            col_tiles,
            frame_count,
            row_count,
            TW,
        )

    def forward(head_index):
        offset = head_index * head_width
        allowed = head_mask(head_index)
        query_head = lax.dynamic_slice_in_dim(own_q, offset, head_width, 2)
        cot_head = lax.dynamic_slice_in_dim(own_c, offset, head_width, 2)
        key_region = region_rows(lax.dynamic_slice_in_dim(key_pad, offset, head_width, 3), TW)
        text_head = lax.dynamic_slice_in_dim(text_keys, offset, head_width, 1)
        image_scores, log_total, text_part = forward_head(
            query_head, key_region, text_head, cot_head, allowed, score_scale
        )
        image_probs = jnp.exp(image_scores - log_total[..., None]).astype(jnp.bfloat16)
        spread = jnp.einsum(
            "cql,cqd->cld", image_probs, cot_head, preferred_element_type=jnp.float32
        )
        return (text_part, place_back(spread, frame_count, row_count, TW))

    text_part, head_out = lax.map(forward, head_ids)
    text_value = jnp.transpose(text_part, (1, 0, 2)).reshape(-1, value_width)
    middle = head_out[:, :, row_count : 2 * row_count]
    for direction, border in (
        (-1, head_out[:, :, :row_count]),
        (1, head_out[:, :, 2 * row_count :]),
    ):
        middle = middle + shifted(border.astype(jnp.bfloat16), "height", direction).astype(
            border.dtype
        )
    own_part = middle[:, frame_count : 2 * frame_count]
    for direction, border in ((-1, middle[:, :frame_count]), (1, middle[:, 2 * frame_count :])):
        own_part = own_part + shifted(border.astype(jnp.bfloat16), "tm", direction).astype(
            border.dtype
        )
    value_f32 = jnp.transpose(own_part, (1, 2, 3, 0, 4)).reshape(
        frame_count, row_count, col_count, value_width
    )
    value_grad = value_f32.astype(jnp.bfloat16)
    noise_level = timestep[0].astype(jnp.float32) / 1000.0
    mixed = (
        (1.0 - noise_level) * clean_latents.astype(jnp.float32)
        + noise_level * gaussian_noise.astype(jnp.float32)
    ).astype(jnp.bfloat16)
    mixed = mixed.reshape(-1, mixed.shape[3])
    flat_value = value_grad.reshape(-1, value_width)
    hidden = jnp.dot(mixed, down_image, preferred_element_type=jnp.float32).astype(jnp.bfloat16)
    grad_up = lax.dot_general(
        hidden, flat_value, (((0,), (0,)), ((), ())), preferred_element_type=jnp.float32
    )
    backward_low = lax.dot_general(
        flat_value, up_image, (((1,), (1,)), ((), ())), preferred_element_type=jnp.float32
    ).astype(jnp.bfloat16)
    grad_down = lax.dot_general(
        mixed, backward_low, (((0,), (0,)), ((), ())), preferred_element_type=jnp.float32
    )
    text_hidden = jnp.dot(text_states, down_text, preferred_element_type=jnp.float32)
    token_total = frame_count * row_count * col_count * frame_tiles * row_tiles
    param_total = 2 * grad_down.size + 2 * grad_up.size
    sketch_scale = (token_total * (param_total // SKETCH)) ** (-0.5)
    text_down_grad, text_up_grad = text_grads(text_hidden, text_value, text_states, up_text)
    local_sketch = count_sketch(
        (grad_down, grad_up, text_down_grad, text_up_grad), sketch_seed[0], SKETCH, sketch_scale
    )
    grad_sketch = lax.psum(local_sketch, ("tm", "height"))
    return (value_grad, grad_sketch)


def solution(mesh):
    return jax.shard_map(
        per_device,
        mesh=mesh,
        in_specs=(
            P("tm", "height", None, None),
            P("tm", "height", None, None),
            P(),
            P("tm", "height", None, None),
            P("tm", "height", None, None),
            P("tm", "height", None, None),
            P(),
            P(),
            P(),
            P(),
            P(),
            P(),
            P(),
            P(),
        ),
        out_specs=(P("tm", "height", None, None), P()),
        check_vma=False,
    )
```

profile of v0, /device:TPU:1, one launch (start us, length us, event | category | flops | bytes accessed | tf_op | source)
XLA Modules:
  0.0 920.2 jit_solution(15900157499959258757)
XLA Ops:
  7.2 5.1 collective-permute-start
  12.3 1.9 collective-permute-start.1
  14.2 7.3 collective-permute-done
  22.5 2.1 constant_dynamic-update-slice_fusion.1
  28.1 12.5 %collective-permute-start.2 = (bf16[12,4,16,1536]{3,2,1,0:T(8,128)(2,1)}, bf16[12,4,16,1536]{3,2,1,0:T(8,128)(2,1)}, u32[]{:S(2)}, u32[]{:S(2)}) collective-permute-start(bf16[12,4,16,1536]{3,2,1,0:T(8,128)(2,1)} %constant_dynamic-update-slice_fusion), channel_id=1, source_target_pairs={{0,1},{1,2},{2,3},{3,4},{4,5},{5,6},{6,7},{7,8},{8,9},{9,10},{10,1... | collective-permute-start | bytes 7077896 | tf_op jit(solution)/shard_map/ppermute | solution.py:15
  40.7 2.1 copy.51
  42.8 97.1 %collective-permute-done.3 = bf16[12,4,16,1536]{3,2,1,0:T(8,128)(2,1)} collective-permute-done((bf16[12,4,16,1536]{3,2,1,0:T(8,128)(2,1)}, bf16[12,4,16,1536]{3,2,1,0:T(8,128)(2,1)}, u32[]{:S(2)}, u32[]{:S(2)}) %collective-permute-start.3) | collective-permute-done | bytes 2359328 | tf_op jit(solution)/shard_map/ppermute | solution.py:18
  139.9 9.7 %fusion.52 = bf16[12,12,32,1536]{3,2,1,0:T(8,128)(2,1)} fusion(bf16[12,4,16,1536]{3,2,1,0:T(8,128)(2,1)} %collective-permute-done.3, bf16[12,4,16,1536]{3,2,1,0:T(8,128)(2,1)} %constant_dynamic-update-slice_fusion, bf16[12,4,16,1536]{3,2,1,0:T(8,128)(2,1)} %collective-permute-done.2), kind=kLoop, calls=%fused_computation.99 | loop fusion | flops 84934656 | bytes 21233664 | tf_op jit(solution)/shard_map/concatenate | solution.py:19
  149.6 213.1 %while.15 = (s32[]{:T(128)}, f32[12,256,128]{1,2,0:T(8,128)}, f32[12,12,12,16,128]{4,3,2,1,0:T(8,128)}, s32[12]{0:T(128)S(1)}, bf16[2,128,1536]{2,1,0:T(8,128)(2...) while((s32[]{:T(128)}, f32[12,256,128]{1,2,0:T(8,128)}, ...), condition=%wide.region_5.6_spmd, body=%wide.region_0.5_spmd.sunk | while | flops 499376128 | bytes 40042176 | solution.py:185
  169.7 1.9 dynamic-slice_bitcast_fusion.4
  187.6 2.0 dynamic-slice_bitcast_fusion.4
  193.3 1.9 compare_and_fusion.4
  228.6 1.9 compare_and_fusion.4
  258.5 2.0 dynamic-slice_bitcast_fusion.4
  282.0 1.9 compare_and_fusion.4
  347.4 2.0 dynamic-slice_bitcast_fusion.4
  353.1 1.9 compare_and_fusion.4
  362.7 9.7 %convert.8 = bf16[12,12,12,16,128]{4,3,2,1,0:T(8,128)(2,1)} convert(f32[12,12,12,16,128]{4,3,2,1,0:T(8,128)} %get-tuple-element.191) | non-fusion elementwise | flops 3538944 | bytes 21233664 | tf_op jit(solution)/shard_map/convert.3
  372.4 6.3 fusion.75
  378.7 42.7 %collective-permute-start.5 = (bf16[12,12,4,16,128]{4,3,2,1,0:T(8,128)(2,1)}, bf16[12,12,4,16,128]{4,3,2,1,0:T(8,128)(2,1)}, u32[]{:S(2)}, u32[]{:S(2)}) collective-permute-start(bf16[12,12,4,16,128]{4,3,2,1,0:T(8,128)(2,1)} %get-tuple-element.230), channel_id=1, source_target_pairs={{0,1},{1,2},{2,3},{3,4},{4,5},{5,6},{6,7},{7,8},{8,9},{9,10},{10,1... | collective-permute-start | bytes 7077896 | tf_op jit(solution)/shard_map/ppermute | solution.py:26
  424.5 2.6 add_convert_fusion
  427.1 34.4 %collective-permute-done.5 = bf16[12,12,4,16,128]{4,3,2,1,0:T(8,128)(2,1)} collective-permute-done((bf16[12,12,4,16,128]{4,3,2,1,0:T(8,128)(2,1)}, bf16[12,12,4,16,128]{4,3,2,1,0:T(8,128)(2,1)}, u32[]{:S(2)}, u32[]{:S(2)}) %collective-permute-start.5) | collective-permute-done | bytes 2359328 | tf_op jit(solution)/shard_map/ppermute | solution.py:26
  461.5 108.8 %collective-permute-done.4 = bf16[12,12,4,16,128]{4,3,2,1,0:T(8,128)(2,1)} collective-permute-done((bf16[12,12,4,16,128]{4,3,2,1,0:T(8,128)(2,1)}, bf16[12,12,4,16,128]{4,3,2,1,0:T(8,128)(2,1)}, u32[]{:S(2)}, u32[]{:S(2)}) %collective-permute-start.4) | collective-permute-done | bytes 2359328 | tf_op jit(solution)/shard_map/ppermute | solution.py:26
  570.3 7.4 fusion.71
  579.3 61.7 %collective-permute-start.7 = (bf16[12,4,4,16,128]{4,3,2,1,0:T(8,128)(2,1)}, bf16[12,4,4,16,128]{4,3,2,1,0:T(8,128)(2,1)}, u32[]{:S(2)}, u32[]{:S(2)}) collective-permute-start(bf16[12,4,4,16,128]{4,3,2,1,0:T(8,128)(2,1)} %get-tuple-element.232), channel_id=1, source_target_pairs={{0,32},{32,64},{64,96},{96,128},{128,160},{160,192},{192,224},{1,3... | collective-permute-start | bytes 2359304 | tf_op jit(solution)/shard_map/ppermute | solution.py:26
  641.1 2.1 collective-permute-start.6
  644.6 2.0 fusion.77
  650.9 3.8 collective-permute-done.6
  654.7 2.2 fusion.54
  659.3 2.2 fusion.55
  662.2 3.7 fusion.56
  672.2 239.7 %all-reduce.5.cloned.1.call-done = f32[16384]{0:T(1024)} async-done(((f32[16384]{0:T(1024)}), f32[16384]{0:T(1024)}) %all-reduce.5.cloned.1.call-update) | async-done | bytes 65552 | tf_op jit(solution)/shard_map/psum | solution.py:229
  (328 shorter events, 190.9 us)
Async XLA Ops:
  7.2 416.8 %copy-start = (bf16[256,3072]{1,0:T(8,128)(2,1)S(1)}, bf16[256,3072]{1,0:T(8,128)(2,1)}, u32[]{:S(2)}) copy-start(bf16[256,3072]{1,0:T(8,128)(2,1)} %param.18) | copy-start | bytes 4718596
  7.2 33.5 %copy-start.6 = (bf16[4,4,16,1536]{3,2,1,0:T(8,128)(2,1)S(1)}, bf16[4,4,16,1536]{3,2,1,0:T(8,128)(2,1)}, u32[]{:S(2)}) copy-start(bf16[4,4,16,1536]{3,2,1,0:T(8,128)(2,1)} %param.19) | copy-start | bytes 2359300
  7.2 904.7 %all-reduce.5.cloned.1.call-start = ((), (), s32[]{:S(2)}) async-start(), calls=%async_computation | async-start | bytes 131072 | tf_op jit(solution)/shard_map/psum | solution.py:229
  7.2 14.3 %collective-permute-start = (bf16[4,4,16,1536]{3,2,1,0:T(8,128)(2,1)}, bf16[4,4,16,1536]{3,2,1,0:T(8,128)(2,1)S(1)}, u32[]{:S(2)}, u32[]{:S(2)}) collective-permute-start(bf16[4,4,16,1536]{3,2,1,0:T(8,128)(2,1)} %param.20), channel_id=1, source_target_pairs={{0,32},{32,64},{64,96},{96,128},{128,160},{160,192},{192,224},{1,3... | collective-permute-start | bytes 2359304 | tf_op jit(solution)/shard_map/ppermute | solution.py:15
  12.3 13.5 %collective-permute-start.1 = (bf16[4,4,16,1536]{3,2,1,0:T(8,128)(2,1)}, bf16[4,4,16,1536]{3,2,1,0:T(8,128)(2,1)S(1)}, u32[]{:S(2)}, u32[]{:S(2)}) collective-permute-start(bf16[4,4,16,1536]{3,2,1,0:T(8,128)(2,1)} %param.20), channel_id=1, source_target_pairs={{32,0},{64,32},{96,64},{128,96},{160,128},{192,160},{224,192},{33,... | collective-permute-start | bytes 2359304 | tf_op jit(solution)/shard_map/ppermute | solution.py:18
  26.8 113.1 %collective-permute-start.3 = (bf16[12,4,16,1536]{3,2,1,0:T(8,128)(2,1)}, bf16[12,4,16,1536]{3,2,1,0:T(8,128)(2,1)}, u32[]{:S(2)}, u32[]{:S(2)}) collective-permute-start(bf16[12,4,16,1536]{3,2,1,0:T(8,128)(2,1)} %constant_dynamic-update-slice_fusion), channel_id=1, source_target_pairs={{1,0},{2,1},{3,2},{4,3},{5,4},{6,5},{7,6},{8,7},{9,8},{10,9},{11,1... | collective-permute-start | bytes 7077896 | tf_op jit(solution)/shard_map/ppermute | solution.py:18
  28.1 111.8 %collective-permute-start.2 = (bf16[12,4,16,1536]{3,2,1,0:T(8,128)(2,1)}, bf16[12,4,16,1536]{3,2,1,0:T(8,128)(2,1)}, u32[]{:S(2)}, u32[]{:S(2)}) collective-permute-start(bf16[12,4,16,1536]{3,2,1,0:T(8,128)(2,1)} %constant_dynamic-update-slice_fusion), channel_id=1, source_target_pairs={{0,1},{1,2},{2,3},{3,4},{4,5},{5,6},{6,7},{7,8},{8,9},{9,10},{10,1... | collective-permute-start | bytes 7077896 | tf_op jit(solution)/shard_map/ppermute | solution.py:15
  42.8 106.8 %copy-start.9 = (s32[12,3]{0,1:T(4,128)S(1)}, s32[12,3]{0,1:T(4,128)}, u32[]{:S(2)}) copy-start(s32[12,3]{0,1:T(4,128)} %param.23) | copy-start | bytes 436
  149.6 4.3 copy-start.4
  167.3 4.4 copy-start.4
  183.8 1.2 copy-start.5
  185.1 4.5 copy-start.4
  202.9 4.3 copy-start.4
  220.6 4.3 copy-start.4
  238.3 4.3 copy-start.4
  256.1 4.5 copy-start.4
  272.7 1.2 copy-start.5
  273.9 4.3 copy-start.4
  291.6 4.3 copy-start.4
  309.3 4.4 copy-start.4
  325.9 1.3 copy-start.5
  327.1 4.4 copy-start.4
  344.9 4.4 copy-start.4
  372.4 51.6 %copy-start.8 = (bf16[3072,16]{0,1:T(8,128)(2,1)S(1)}, bf16[3072,16]{0,1:T(8,128)(2,1)}, u32[]{:S(2)}) copy-start(bf16[3072,16]{0,1:T(8,128)(2,1)} %param.28) | copy-start | bytes 294916
  378.7 82.8 %collective-permute-start.5 = (bf16[12,12,4,16,128]{4,3,2,1,0:T(8,128)(2,1)}, bf16[12,12,4,16,128]{4,3,2,1,0:T(8,128)(2,1)}, u32[]{:S(2)}, u32[]{:S(2)}) collective-permute-start(bf16[12,12,4,16,128]{4,3,2,1,0:T(8,128)(2,1)} %get-tuple-element.230), channel_id=1, source_target_pairs={{0,1},{1,2},{2,3},{3,4},{4,5},{5,6},{6,7},{7,8},{8,9},{9,10},{10,1... | collective-permute-start | bytes 7077896 | tf_op jit(solution)/shard_map/ppermute | solution.py:26
  421.4 148.9 %collective-permute-start.4 = (bf16[12,12,4,16,128]{4,3,2,1,0:T(8,128)(2,1)}, bf16[12,12,4,16,128]{4,3,2,1,0:T(8,128)(2,1)}, u32[]{:S(2)}, u32[]{:S(2)}) collective-permute-start(bf16[12,12,4,16,128]{4,3,2,1,0:T(8,128)(2,1)} %get-tuple-element.229), channel_id=1, source_target_pairs={{1,0},{2,1},{3,2},{4,3},{5,4},{6,5},{7,6},{8,7},{9,8},{10,9},{11,1... | collective-permute-start | bytes 7077896 | tf_op jit(solution)/shard_map/ppermute | solution.py:26
  577.7 65.5 %copy-start.3 = (f32[12,256,128]{1,2,0:T(8,128)S(1)}, f32[12,256,128]{1,2,0:T(8,128)}, u32[]{:S(2)}) copy-start(f32[12,256,128]{1,2,0:T(8,128)} %get-tuple-element.192) | copy-start | bytes 4718596
  577.7 66.9 %copy-start.10 = (bf16[16,1536]{1,0:T(8,128)(2,1)S(1)}, bf16[16,1536]{1,0:T(8,128)(2,1)}, u32[]{:S(2)}) copy-start(bf16[16,1536]{1,0:T(8,128)(2,1)} %param.29) | copy-start | bytes 147460
  579.3 71.6 %collective-permute-start.7 = (bf16[12,4,4,16,128]{4,3,2,1,0:T(8,128)(2,1)}, bf16[12,4,4,16,128]{4,3,2,1,0:T(8,128)(2,1)}, u32[]{:S(2)}, u32[]{:S(2)}) collective-permute-start(bf16[12,4,4,16,128]{4,3,2,1,0:T(8,128)(2,1)} %get-tuple-element.232), channel_id=1, source_target_pairs={{0,32},{32,64},{64,96},{96,128},{128,160},{160,192},{192,224},{1,3... | collective-permute-start | bytes 2359304 | tf_op jit(solution)/shard_map/ppermute | solution.py:26
  641.1 13.6 %collective-permute-start.6 = (bf16[12,4,4,16,128]{4,3,2,1,0:T(8,128)(2,1)}, bf16[12,4,4,16,128]{4,3,2,1,0:T(8,128)(2,1)}, u32[]{:S(2)}, u32[]{:S(2)}) collective-permute-start(bf16[12,4,4,16,128]{4,3,2,1,0:T(8,128)(2,1)} %get-tuple-element.231), channel_id=1, source_target_pairs={{32,0},{64,32},{96,64},{128,96},{160,128},{192,160},{224,192},{33,... | collective-permute-start | bytes 2359304 | tf_op jit(solution)/shard_map/ppermute | solution.py:26
  662.2 5.5 copy-start.7
  667.7 3.5 copy-start.2
  (10 other events, 11.9 us)
Sparse Core Ops, SparseCore 0:
  671.3 240.5 all-reduce.4
where the time goes:
time: 925 us; the launch traced here: 920 us
  waiting for transfers between devices  492 us (53%)
  starting transfers between devices  129 us (14%)
  matrix products  89.3 us (10%)
  other arithmetic  82 us (9%)
  local copies, waits for them, and re-layouts  81.4 us (9%)
  loops' own time  31 us (3%)
  between operations  15.5 us (2%)
    psum x1, waiting for transfers between devices, per_device(): grad_sketch = lax.psum(local_sketch, ('tm', 'height'))  240 us
    ppermute x4, waiting for transfers between devices, shifted(): return lax.ppermute(array, axis, pairs)  147 us
    ppermute x4, starting transfers between devices, shifted(): return lax.ppermute(array, axis, pairs)  108 us
    ppermute x2, waiting for transfers between devices, padded_2(): lax.ppermute(lax.slice_in_dim(block, 0, width, axis=dim), axis, backward)  98.3 us
    reshape x50, local copies, waits for them, and re-layouts, tile_rows(): shaped = block.reshape((frame_count, row_count, col_tiles, width) + rest)  38.7 us
    another operation x1, loops' own time, per_device(): text_part, head_out = lax.map(forward, head_ids)  31 us
    and x12, other arithmetic, window_mask(): inside & (row_tile + row_step >= 0) & (row_tile + row_step < row_tiles)  23 us
    dot_general x12, matrix products, forward(): jnp.einsum('cql,cqd->cld', image_probs, cot_head, preferred_element_type=...  22.2 us
  transfers between devices with their start and end apart: 9, of which 7 were waited for; matrix products, arithmetic and copies ran while one was open for 2% of the time, Pallas kernels for 0%

commit v1 on v0

--- a/solution.py
+++ b/solution.py
@@ -226,7 +226,7 @@
     local_sketch = count_sketch(
         (grad_down, grad_up, text_down_grad, text_up_grad), sketch_seed[0], SKETCH, sketch_scale
     )
-    grad_sketch = lax.psum(local_sketch, ("tm", "height"))
+    grad_sketch = lax.psum(lax.psum(local_sketch, axis_name="height"), axis_name="tm")
     return (value_grad, grad_sketch)
 
 

time: 925 us -> 1150 us (1.24)
  waiting for transfers between devices: 492 us -> 716 us
    psum x1 -> x2, waiting for transfers between devices: 240 us -> 463 us  [the longest x1 378 us: per_device(): lax.psum(local_sketch, axis_name='height')]
  transfers between devices with their start and end apart: 9 -> 10, of which waited for: 7 -> 8; matrix products, arithmetic and copies ran while one was open for 2% -> 1% of each run, Pallas kernels for 0% -> 0%
where the time goes in v1:
time: 1150 us; the launch traced here: 1140 us
  waiting for transfers between devices  716 us (62%)
  starting transfers between devices  129 us (11%)
  matrix products  89.3 us (8%)
  other arithmetic  82 us (7%)
  local copies, waits for them, and re-layouts  81.4 us (7%)
  loops' own time  31 us (3%)
  between operations  15.6 us (1%)
    psum x1, waiting for transfers between devices, per_device(): lax.psum(local_sketch, axis_name='height')  378 us
    ppermute x4, waiting for transfers between devices, shifted(): return lax.ppermute(array, axis, pairs)  147 us
    ppermute x4, starting transfers between devices, shifted(): return lax.ppermute(array, axis, pairs)  108 us
    ppermute x2, waiting for transfers between devices, padded_2(): lax.ppermute(lax.slice_in_dim(block, 0, width, axis=dim), axis, backward)  98.3 us
    psum x1, waiting for transfers between devices, per_device(): lax.psum(lax.psum(local_sketch, axis_name='height'), axis_name='tm')  85.6 us
    reshape x50, local copies, waits for them, and re-layouts, tile_rows(): shaped = block.reshape((frame_count, row_count, col_tiles, width) + rest)  38.7 us
    another operation x1, loops' own time, per_device(): text_part, head_out = lax.map(forward, head_ids)  31 us
    and x12, other arithmetic, window_mask(): inside & (row_tile + row_step >= 0) & (row_tile + row_step < row_tiles)  23 us
  transfers between devices with their start and end apart: 10, of which 8 were waited for; matrix products, arithmetic and copies ran while one was open for 1% of the time, Pallas kernels for 0%

profile of v1, /device:TPU:1, one launch (start us, length us, event | category | flops | bytes accessed | tf_op | source)
XLA Modules:
  0.0 1143.8 jit_solution(15439428069263182074)
XLA Ops:
  7.2 5.1 collective-permute-start
  12.3 1.9 collective-permute-start.1
  14.2 7.3 collective-permute-done
  22.5 2.1 constant_dynamic-update-slice_fusion.1
  28.1 12.5 %collective-permute-start.2 = (bf16[12,4,16,1536]{3,2,1,0:T(8,128)(2,1)}, bf16[12,4,16,1536]{3,2,1,0:T(8,128)(2,1)}, u32[]{:S(2)}, u32[]{:S(2)}) collective-permute-start(bf16[12,4,16,1536]{3,2,1,0:T(8,128)(2,1)} %constant_dynamic-update-slice_fusion), channel_id=1, source_target_pairs={{0,1},{1,2},{2,3},{3,4},{4,5},{5,6},{6,7},{7,8},{8,9},{9,10},{10,1... | collective-permute-start | bytes 7077896 | tf_op jit(solution)/shard_map/ppermute | solution.py:15
  40.7 2.1 copy.51
  42.8 97.1 %collective-permute-done.3 = bf16[12,4,16,1536]{3,2,1,0:T(8,128)(2,1)} collective-permute-done((bf16[12,4,16,1536]{3,2,1,0:T(8,128)(2,1)}, bf16[12,4,16,1536]{3,2,1,0:T(8,128)(2,1)}, u32[]{:S(2)}, u32[]{:S(2)}) %collective-permute-start.3) | collective-permute-done | bytes 2359328 | tf_op jit(solution)/shard_map/ppermute | solution.py:18
  139.9 9.7 fusion.52
  149.6 213.1 %while.15 = (s32[]{:T(128)}, f32[12,256,128]{1,2,0:T(8,128)}, f32[12,12,12,16,128]{4,3,2,1,0:T(8,128)}, s32[12]{0:T(128)S(1)}, bf16[2,128,1536]{2,1,0:T(8,128)(2...) while((s32[]{:T(128)}, f32[12,256,128]{1,2,0:T(8,128)}, ...), condition=%wide.region_5.6_spmd, body=%wide.region_0.5_spmd.sunk | while | flops 499376128 | bytes 40042176 | solution.py:185
  169.7 1.9 dynamic-slice_bitcast_fusion.4
  187.6 2.0 dynamic-slice_bitcast_fusion.4
  193.3 1.9 compare_and_fusion.4
  228.6 1.9 compare_and_fusion.4
  258.5 2.0 dynamic-slice_bitcast_fusion.4
  282.0 1.9 compare_and_fusion.4
  347.4 2.0 dynamic-slice_bitcast_fusion.4
  362.7 9.7 convert.8
  372.4 6.3 fusion.75
  378.7 42.7 %collective-permute-start.5 = (bf16[12,12,4,16,128]{4,3,2,1,0:T(8,128)(2,1)}, bf16[12,12,4,16,128]{4,3,2,1,0:T(8,128)(2,1)}, u32[]{:S(2)}, u32[]{:S(2)}) collective-permute-start(bf16[12,12,4,16,128]{4,3,2,1,0:T(8,128)(2,1)} %get-tuple-element.230), channel_id=1, source_target_pairs={{0,1},{1,2},{2,3},{3,4},{4,5},{5,6},{6,7},{7,8},{8,9},{9,10},{10,1... | collective-permute-start | bytes 7077896 | tf_op jit(solution)/shard_map/ppermute | solution.py:26
  424.5 2.6 add_convert_fusion
  427.1 34.4 %collective-permute-done.5 = bf16[12,12,4,16,128]{4,3,2,1,0:T(8,128)(2,1)} collective-permute-done((bf16[12,12,4,16,128]{4,3,2,1,0:T(8,128)(2,1)}, bf16[12,12,4,16,128]{4,3,2,1,0:T(8,128)(2,1)}, u32[]{:S(2)}, u32[]{:S(2)}) %collective-permute-start.5) | collective-permute-done | bytes 2359328 | tf_op jit(solution)/shard_map/ppermute | solution.py:26
  461.5 108.8 %collective-permute-done.4 = bf16[12,12,4,16,128]{4,3,2,1,0:T(8,128)(2,1)} collective-permute-done((bf16[12,12,4,16,128]{4,3,2,1,0:T(8,128)(2,1)}, bf16[12,12,4,16,128]{4,3,2,1,0:T(8,128)(2,1)}, u32[]{:S(2)}, u32[]{:S(2)}) %collective-permute-start.4) | collective-permute-done | bytes 2359328 | tf_op jit(solution)/shard_map/ppermute | solution.py:26
  570.3 7.4 fusion.71
  579.3 61.7 %collective-permute-start.7 = (bf16[12,4,4,16,128]{4,3,2,1,0:T(8,128)(2,1)}, bf16[12,4,4,16,128]{4,3,2,1,0:T(8,128)(2,1)}, u32[]{:S(2)}, u32[]{:S(2)}) collective-permute-start(bf16[12,4,4,16,128]{4,3,2,1,0:T(8,128)(2,1)} %get-tuple-element.232), channel_id=1, source_target_pairs={{0,32},{32,64},{64,96},{96,128},{128,160},{160,192},{192,224},{1,3... | collective-permute-start | bytes 2359304 | tf_op jit(solution)/shard_map/ppermute | solution.py:26
  641.1 2.1 collective-permute-start.6
  644.6 2.0 fusion.77
  650.9 3.8 collective-permute-done.6
  654.7 2.2 fusion.54
  659.3 2.2 fusion.55
  662.2 3.7 fusion.56
  671.2 377.6 %all-reduce.6.cloned.1.call-done = f32[16384]{0:T(1024)} async-done(((f32[16384]{0:T(1024)}), f32[16384]{0:T(1024)}) %all-reduce.6.cloned.1.call-update) | async-done | bytes 65552 | tf_op jit(solution)/shard_map/psum | solution.py:229
  1049.8 85.6 %all-reduce.8.cloned.1.call-done = f32[16384]{0:T(1024)} async-done(((f32[16384]{0:T(1024)}), f32[16384]{0:T(1024)}) %all-reduce.8.cloned.1.call-update) | async-done | bytes 65552 | tf_op jit(solution)/shard_map/psum | solution.py:229
  (331 shorter events, 192.9 us)
Async XLA Ops:
  7.2 416.8 %copy-start = (bf16[256,3072]{1,0:T(8,128)(2,1)S(1)}, bf16[256,3072]{1,0:T(8,128)(2,1)}, u32[]{:S(2)}) copy-start(bf16[256,3072]{1,0:T(8,128)(2,1)} %param.18) | copy-start | bytes 4718596
  7.2 33.5 %copy-start.6 = (bf16[4,4,16,1536]{3,2,1,0:T(8,128)(2,1)S(1)}, bf16[4,4,16,1536]{3,2,1,0:T(8,128)(2,1)}, u32[]{:S(2)}) copy-start(bf16[4,4,16,1536]{3,2,1,0:T(8,128)(2,1)} %param.19) | copy-start | bytes 2359300
  7.2 1041.6 %all-reduce.6.cloned.1.call-start = ((), (), s32[]{:S(2)}) async-start(), calls=%async_computation | async-start | bytes 131072 | tf_op jit(solution)/shard_map/psum | solution.py:229
  7.2 14.3 %collective-permute-start = (bf16[4,4,16,1536]{3,2,1,0:T(8,128)(2,1)}, bf16[4,4,16,1536]{3,2,1,0:T(8,128)(2,1)S(1)}, u32[]{:S(2)}, u32[]{:S(2)}) collective-permute-start(bf16[4,4,16,1536]{3,2,1,0:T(8,128)(2,1)} %param.20), channel_id=1, source_target_pairs={{0,32},{32,64},{64,96},{96,128},{128,160},{160,192},{192,224},{1,3... | collective-permute-start | bytes 2359304 | tf_op jit(solution)/shard_map/ppermute | solution.py:15
  12.3 13.5 %collective-permute-start.1 = (bf16[4,4,16,1536]{3,2,1,0:T(8,128)(2,1)}, bf16[4,4,16,1536]{3,2,1,0:T(8,128)(2,1)S(1)}, u32[]{:S(2)}, u32[]{:S(2)}) collective-permute-start(bf16[4,4,16,1536]{3,2,1,0:T(8,128)(2,1)} %param.20), channel_id=1, source_target_pairs={{32,0},{64,32},{96,64},{128,96},{160,128},{192,160},{224,192},{33,... | collective-permute-start | bytes 2359304 | tf_op jit(solution)/shard_map/ppermute | solution.py:18
  26.8 113.1 %collective-permute-start.3 = (bf16[12,4,16,1536]{3,2,1,0:T(8,128)(2,1)}, bf16[12,4,16,1536]{3,2,1,0:T(8,128)(2,1)}, u32[]{:S(2)}, u32[]{:S(2)}) collective-permute-start(bf16[12,4,16,1536]{3,2,1,0:T(8,128)(2,1)} %constant_dynamic-update-slice_fusion), channel_id=1, source_target_pairs={{1,0},{2,1},{3,2},{4,3},{5,4},{6,5},{7,6},{8,7},{9,8},{10,9},{11,1... | collective-permute-start | bytes 7077896 | tf_op jit(solution)/shard_map/ppermute | solution.py:18
  28.1 111.8 %collective-permute-start.2 = (bf16[12,4,16,1536]{3,2,1,0:T(8,128)(2,1)}, bf16[12,4,16,1536]{3,2,1,0:T(8,128)(2,1)}, u32[]{:S(2)}, u32[]{:S(2)}) collective-permute-start(bf16[12,4,16,1536]{3,2,1,0:T(8,128)(2,1)} %constant_dynamic-update-slice_fusion), channel_id=1, source_target_pairs={{0,1},{1,2},{2,3},{3,4},{4,5},{5,6},{6,7},{7,8},{8,9},{9,10},{10,1... | collective-permute-start | bytes 7077896 | tf_op jit(solution)/shard_map/ppermute | solution.py:15
  42.8 106.8 %copy-start.9 = (s32[12,3]{0,1:T(4,128)S(1)}, s32[12,3]{0,1:T(4,128)}, u32[]{:S(2)}) copy-start(s32[12,3]{0,1:T(4,128)} %param.23) | copy-start | bytes 436
  149.6 4.3 copy-start.4
  167.3 4.4 copy-start.4
  185.1 4.5 copy-start.4
  202.9 4.3 copy-start.4
  220.6 4.3 copy-start.4
  238.3 4.3 copy-start.4
  256.1 4.5 copy-start.4
  272.7 1.2 copy-start.5
  273.9 4.3 copy-start.4
  291.6 4.3 copy-start.4
  309.3 4.4 copy-start.4
  325.9 1.3 copy-start.5
  327.1 4.4 copy-start.4
  344.9 4.4 copy-start.4
  372.4 51.6 %copy-start.8 = (bf16[3072,16]{0,1:T(8,128)(2,1)S(1)}, bf16[3072,16]{0,1:T(8,128)(2,1)}, u32[]{:S(2)}) copy-start(bf16[3072,16]{0,1:T(8,128)(2,1)} %param.28) | copy-start | bytes 294916
  378.7 82.8 %collective-permute-start.5 = (bf16[12,12,4,16,128]{4,3,2,1,0:T(8,128)(2,1)}, bf16[12,12,4,16,128]{4,3,2,1,0:T(8,128)(2,1)}, u32[]{:S(2)}, u32[]{:S(2)}) collective-permute-start(bf16[12,12,4,16,128]{4,3,2,1,0:T(8,128)(2,1)} %get-tuple-element.230), channel_id=1, source_target_pairs={{0,1},{1,2},{2,3},{3,4},{4,5},{5,6},{6,7},{7,8},{8,9},{9,10},{10,1... | collective-permute-start | bytes 7077896 | tf_op jit(solution)/shard_map/ppermute | solution.py:26
  421.4 148.9 %collective-permute-start.4 = (bf16[12,12,4,16,128]{4,3,2,1,0:T(8,128)(2,1)}, bf16[12,12,4,16,128]{4,3,2,1,0:T(8,128)(2,1)}, u32[]{:S(2)}, u32[]{:S(2)}) collective-permute-start(bf16[12,12,4,16,128]{4,3,2,1,0:T(8,128)(2,1)} %get-tuple-element.229), channel_id=1, source_target_pairs={{1,0},{2,1},{3,2},{4,3},{5,4},{6,5},{7,6},{8,7},{9,8},{10,9},{11,1... | collective-permute-start | bytes 7077896 | tf_op jit(solution)/shard_map/ppermute | solution.py:26
  577.7 65.5 %copy-start.3 = (f32[12,256,128]{1,2,0:T(8,128)S(1)}, f32[12,256,128]{1,2,0:T(8,128)}, u32[]{:S(2)}) copy-start(f32[12,256,128]{1,2,0:T(8,128)} %get-tuple-element.192) | copy-start | bytes 4718596
  577.7 66.9 %copy-start.10 = (bf16[16,1536]{1,0:T(8,128)(2,1)S(1)}, bf16[16,1536]{1,0:T(8,128)(2,1)}, u32[]{:S(2)}) copy-start(bf16[16,1536]{1,0:T(8,128)(2,1)} %param.29) | copy-start | bytes 147460
  579.3 71.6 %collective-permute-start.7 = (bf16[12,4,4,16,128]{4,3,2,1,0:T(8,128)(2,1)}, bf16[12,4,4,16,128]{4,3,2,1,0:T(8,128)(2,1)}, u32[]{:S(2)}, u32[]{:S(2)}) collective-permute-start(bf16[12,4,4,16,128]{4,3,2,1,0:T(8,128)(2,1)} %get-tuple-element.232), channel_id=1, source_target_pairs={{0,32},{32,64},{64,96},{96,128},{128,160},{160,192},{192,224},{1,3... | collective-permute-start | bytes 2359304 | tf_op jit(solution)/shard_map/ppermute | solution.py:26
  641.1 13.6 %collective-permute-start.6 = (bf16[12,4,4,16,128]{4,3,2,1,0:T(8,128)(2,1)}, bf16[12,4,4,16,128]{4,3,2,1,0:T(8,128)(2,1)}, u32[]{:S(2)}, u32[]{:S(2)}) collective-permute-start(bf16[12,4,4,16,128]{4,3,2,1,0:T(8,128)(2,1)} %get-tuple-element.231), channel_id=1, source_target_pairs={{32,0},{64,32},{96,64},{128,96},{160,128},{192,160},{224,192},{33,... | collective-permute-start | bytes 2359304 | tf_op jit(solution)/shard_map/ppermute | solution.py:26
  662.2 5.5 copy-start.7
  667.7 381.1 %copy-start.2 = (bf16[12,4,4,16,128]{4,3,2,1,0:T(8,128)(2,1)S(1)}, bf16[12,4,4,16,128]{4,3,2,1,0:T(8,128)(2,1)}, u32[]{:S(2)}) copy-start(bf16[12,4,4,16,128]{4,3,2,1,0:T(8,128)(2,1)} %copy-done.1) | copy-start | bytes 2359300
  671.2 464.3 %all-reduce.8.cloned.1.call-start = ((), (), s32[]{:S(2)}) async-start(), calls=%async_computation.1 | async-start | bytes 131072 | tf_op jit(solution)/shard_map/psum | solution.py:229
  (11 other events, 13.2 us)
Sparse Core Ops, SparseCore 0:
  671.3 377.4 all-reduce.5
  1051.6 83.8 all-reduce.7
